TPU v7x, 256 devices: a whole 4x4x8 slice. The times are simulated.
256 devices in a mesh: blk: 32 (over z, x_lo, core), pool: 8 (over x_hi, y).
Axes of the slice: x: 4 (x_hi: 2, x_lo: 2; x = x_hi * 2 + x_lo), y: 4, z: 8, core: 2. Of those that a mesh axis runs over, the one named last changes fastest.
Arguments:
- queries: bfloat16 [256, 128, 128], P('blk', 'pool'), may hold values from -5 to 5
- kv_cache: bfloat16 [8, 6144, 16, 256], P(None, ('blk', 'pool')), may hold values from -6 to 6
- block_owner: int32 [3072, 1], P('blk'), may hold values from 0 to 7; in each aligned block of 96 rows (0 to 95, 96 to 191, ...) at most 24 rows name the same one
Outputs:
- attended: bfloat16 [256, 128, 128], P('blk', 'pool')
Inputs may be any that keep to these rules, and one draw needn't show every extreme that they name: `block_owner`: in the rows of one holder (aligned blocks of 96 rows) no owner is named more than 24 times; in some holders one owner is named exactly 24 times.
All inputs are finite; a program needn't handle non-finite values.
Results may differ from a plain program's by a relative error of at most 0.0047.
Values may be sent and summed in bfloat16 or wider, within the bound.
A program may use at most 64 MiB of HBM per device.

v0:
```python
import math

import jax
import jax.numpy as jnp
from jax import lax
from jax.sharding import PartitionSpec as P


def shifted(block, axis, distance):
    devices = range(lax.axis_size(axis))
    route = [((i - distance) % len(devices), i) for i in devices]
    return lax.ppermute(block, axis, route)


def slice_attend(query_matrix, common_prefix, valid_tokens):
    head_extent = query_matrix.shape[-1]
    attention_logits = jnp.einsum(
        "hun,hwn->huw",
        query_matrix,
        common_prefix[:, :, :head_extent],
        preferred_element_type=jnp.float32,
    ) * (1.0 / math.sqrt(head_extent))
    attention_logits = jnp.where(valid_tokens[None, None, :], attention_logits, -1e30)
    maxima = jnp.max(attention_logits, axis=-1)
    exponent = jnp.exp(attention_logits - maxima[..., None])
    totals = jnp.sum(exponent, axis=-1)
    softmax_weights = exponent.astype(jnp.bfloat16)
    weighted_values = jnp.einsum(
        "bzv,bvn->bzn",
        softmax_weights,
        common_prefix[:, :, head_extent:],
        preferred_element_type=jnp.float32,
    )
    return (maxima, totals, weighted_values)


def combine_states(running, fresh):
    old_max, old_tot, old_sum = running
    new_max, new_tot, new_sum = fresh
    largest = jnp.maximum(old_max, new_max)
    keep_old = jnp.exp(old_max - largest)
    keep_new = jnp.exp(new_max - largest)
    return (
        largest,
        old_tot * keep_old + new_tot * keep_new,
        old_sum * keep_old[..., None] + new_sum * keep_new[..., None],
    )


def body(queries, kv_cache, block_owner):
    pool_n = lax.axis_size("pool")
    blk_n = lax.axis_size("blk")
    req_dev, heads_dev, head_extent = queries.shape
    kv_heads, capacity, block_len, row_width = kv_cache.shape
    kvh_dev = kv_heads // pool_n
    group_size = heads_dev // kvh_dev
    owner_ids = block_owner[:, 0]
    owner_counts = jnp.sum(
        (owner_ids[:, None] == jnp.arange(pool_n, dtype=jnp.int32)[None, :]).astype(jnp.int32),
        axis=0,
    )
    live_slots = jnp.arange(capacity, dtype=jnp.int32)[None, :] < owner_counts[:, None]
    valid_tokens = jnp.broadcast_to(live_slots[:, :, None], (pool_n, capacity, block_len)).reshape(
        pool_n * capacity * block_len
    )
    grouped = kv_cache.reshape(pool_n, kvh_dev, capacity, block_len, row_width)
    fetched = lax.all_to_all(grouped, "pool", split_axis=0, concat_axis=2, tiled=True)
    common_prefix = fetched.reshape(kvh_dev, pool_n * capacity * block_len, row_width)
    query_matrix = queries.reshape(req_dev, kvh_dev, group_size, head_extent).transpose(1, 0, 2, 3)
    query_matrix = query_matrix.reshape(kvh_dev, req_dev * group_size, head_extent)
    row_count = req_dev * group_size
    start_state = (
        jnp.full((kvh_dev, row_count), -1e30, jnp.float32),
        jnp.zeros((kvh_dev, row_count), jnp.float32),
        jnp.zeros((kvh_dev, row_count, head_extent), jnp.float32),
    )

    def turn(turn_index, carried):
        moving, running = carried
        running = combine_states(running, slice_attend(moving, common_prefix, valid_tokens))
        moving = shifted(moving, "blk", 1)
        running = shifted((running[0], running[1], running[2]), "blk", 1)
        return (moving, running)

    moving, running = lax.fori_loop(0, blk_n, turn, (query_matrix, start_state))
    largest, norm, combined = running
    attended = (combined / norm[..., None]).astype(jnp.bfloat16)
    attended = attended.reshape(kvh_dev, req_dev, group_size, head_extent).transpose(1, 0, 2, 3)
    return attended.reshape(req_dev, heads_dev, head_extent)


def solution(mesh):
    in_specs = (P("blk", "pool", None), P(None, ("blk", "pool"), None, None), P("blk", None))
    out_specs = P("blk", "pool", None)
    return jax.shard_map(body, mesh=mesh, in_specs=in_specs, out_specs=out_specs, check_vma=False)
```

profile of v0, /device:TPU:4, one launch (start us, length us, event | category | flops | bytes accessed | tf_op | source)
XLA Modules:
  0.0 280.4 jit_solution(10501624249685958736)
XLA Ops:
  0.0 7.6 %all-to-all-start = ((bf16[8,1,24,16,256]{4,3,2,1,0:T(8,128)(2,1)}), bf16[8,1,24,16,256]{4,3,2,1,0:T(8,128)(2,1)S(1)}, u32[]{:S(2)}, u32[]{:S(2)}) async-start(bf16[8,1,24,16,256]{4,3,2,1,0:T(8,128)(2,1)} %bitcast.59), calls=%async_computation | async-start | bytes 3145728 | tf_op jit(solution)/shard_map/all_to_all | solution.py:67
  7.8 19.7 %all-to-all-done = bf16[8,1,24,16,256]{4,3,2,1,0:T(8,128)(2,1)S(1)} async-done(((bf16[8,1,24,16,256]{4,3,2,1,0:T(8,128)(2,1)}), bf16[8,1,24,16,256]{4,3,2,1,0:T(8,128)(2,1)S(1)}, u32[]{:S(2)}, u32[]{:S(2)}) %all-to-all-start) | async-done | bytes 1572896 | tf_op jit(solution)/shard_map/all_to_all | solution.py:67
  27.5 252.2 %while.17 = (s32[]{:T(128)}, bf16[1,128,128]{2,1,0:T(8,128)(2,1)S(1)}, f32[1,128]{1,0:T(1,128)S(1)}, f32[1,128]{1,0:T(1,128)S(1)}, f32[1,128,128]{2,1,0:T(8,128)...) while((s32[]{:T(128)}, bf16[1,128,128]{2,1,0:T(8,128)(2,1)S(1)}, ...), condition=%wide.region_4.5_spmd.clone, body=%wide.region_1.4_spmd.clone.sunk | while | flops 204128768 | bytes 6938037 | solution.py:85
  27.7 0.5 fusion.27
  29.1 1.3 collective-permute-start
  30.5 2.2 collective-permute-start.2
  32.7 4.5 %collective-permute-done.1 = f32[1,128]{1,0:T(1,128)S(1)} collective-permute-done((f32[1,128]{1,0:T(1,128)S(1)}, f32[1,128]{1,0:T(1,128)S(1)}, u32[]{:S(2)}, u32[]{:S(2)}) %collective-permute-start.1) | collective-permute-done | bytes 544 | tf_op jit(solution)/shard_map/while/body/eval_jaxpr/ppermute | solution.py:12
  39.0 0.5 collective-permute-start.2
  39.5 5.5 %collective-permute-done.1 = f32[1,128]{1,0:T(1,128)S(1)} collective-permute-done((f32[1,128]{1,0:T(1,128)S(1)}, f32[1,128]{1,0:T(1,128)S(1)}, u32[]{:S(2)}, u32[]{:S(2)}) %collective-permute-start.1) | collective-permute-done | bytes 544 | tf_op jit(solution)/shard_map/while/body/eval_jaxpr/ppermute | solution.py:12
  45.2 0.5 fusion.27
  46.9 5.9 %collective-permute-done.1 = f32[1,128]{1,0:T(1,128)S(1)} collective-permute-done((f32[1,128]{1,0:T(1,128)S(1)}, f32[1,128]{1,0:T(1,128)S(1)}, u32[]{:S(2)}, u32[]{:S(2)}) %collective-permute-start.1) | collective-permute-done | bytes 544 | tf_op jit(solution)/shard_map/while/body/eval_jaxpr/ppermute | solution.py:12
  54.7 5.9 %collective-permute-done.1 = f32[1,128]{1,0:T(1,128)S(1)} collective-permute-done((f32[1,128]{1,0:T(1,128)S(1)}, f32[1,128]{1,0:T(1,128)S(1)}, u32[]{:S(2)}, u32[]{:S(2)}) %collective-permute-start.1) | collective-permute-done | bytes 544 | tf_op jit(solution)/shard_map/while/body/eval_jaxpr/ppermute | solution.py:12
  60.9 0.5 fusion.27
  62.5 5.9 %collective-permute-done.1 = f32[1,128]{1,0:T(1,128)S(1)} collective-permute-done((f32[1,128]{1,0:T(1,128)S(1)}, f32[1,128]{1,0:T(1,128)S(1)}, u32[]{:S(2)}, u32[]{:S(2)}) %collective-permute-start.1) | collective-permute-done | bytes 544 | tf_op jit(solution)/shard_map/while/body/eval_jaxpr/ppermute | solution.py:12
  68.7 0.5 fusion.27
  70.4 5.9 %collective-permute-done.1 = f32[1,128]{1,0:T(1,128)S(1)} collective-permute-done((f32[1,128]{1,0:T(1,128)S(1)}, f32[1,128]{1,0:T(1,128)S(1)}, u32[]{:S(2)}, u32[]{:S(2)}) %collective-permute-start.1) | collective-permute-done | bytes 544 | tf_op jit(solution)/shard_map/while/body/eval_jaxpr/ppermute | solution.py:12
  76.5 0.5 fusion.27
  78.2 5.9 %collective-permute-done.1 = f32[1,128]{1,0:T(1,128)S(1)} collective-permute-done((f32[1,128]{1,0:T(1,128)S(1)}, f32[1,128]{1,0:T(1,128)S(1)}, u32[]{:S(2)}, u32[]{:S(2)}) %collective-permute-start.1) | collective-permute-done | bytes 544 | tf_op jit(solution)/shard_map/while/body/eval_jaxpr/ppermute | solution.py:12
  84.4 0.5 fusion.27
  86.0 5.9 %collective-permute-done.1 = f32[1,128]{1,0:T(1,128)S(1)} collective-permute-done((f32[1,128]{1,0:T(1,128)S(1)}, f32[1,128]{1,0:T(1,128)S(1)}, u32[]{:S(2)}, u32[]{:S(2)}) %collective-permute-start.1) | collective-permute-done | bytes 544 | tf_op jit(solution)/shard_map/while/body/eval_jaxpr/ppermute | solution.py:12
  92.2 0.5 fusion.27
  93.8 5.9 %collective-permute-done.1 = f32[1,128]{1,0:T(1,128)S(1)} collective-permute-done((f32[1,128]{1,0:T(1,128)S(1)}, f32[1,128]{1,0:T(1,128)S(1)}, u32[]{:S(2)}, u32[]{:S(2)}) %collective-permute-start.1) | collective-permute-done | bytes 544 | tf_op jit(solution)/shard_map/while/body/eval_jaxpr/ppermute | solution.py:12
  100.0 0.5 fusion.27
  101.7 5.9 %collective-permute-done.1 = f32[1,128]{1,0:T(1,128)S(1)} collective-permute-done((f32[1,128]{1,0:T(1,128)S(1)}, f32[1,128]{1,0:T(1,128)S(1)}, u32[]{:S(2)}, u32[]{:S(2)}) %collective-permute-start.1) | collective-permute-done | bytes 544 | tf_op jit(solution)/shard_map/while/body/eval_jaxpr/ppermute | solution.py:12
  107.8 0.5 fusion.27
  109.5 5.9 %collective-permute-done.1 = f32[1,128]{1,0:T(1,128)S(1)} collective-permute-done((f32[1,128]{1,0:T(1,128)S(1)}, f32[1,128]{1,0:T(1,128)S(1)}, u32[]{:S(2)}, u32[]{:S(2)}) %collective-permute-start.1) | collective-permute-done | bytes 544 | tf_op jit(solution)/shard_map/while/body/eval_jaxpr/ppermute | solution.py:12
  117.3 5.9 %collective-permute-done.1 = f32[1,128]{1,0:T(1,128)S(1)} collective-permute-done((f32[1,128]{1,0:T(1,128)S(1)}, f32[1,128]{1,0:T(1,128)S(1)}, u32[]{:S(2)}, u32[]{:S(2)}) %collective-permute-start.1) | collective-permute-done | bytes 544 | tf_op jit(solution)/shard_map/while/body/eval_jaxpr/ppermute | solution.py:12
  125.1 5.9 %collective-permute-done.1 = f32[1,128]{1,0:T(1,128)S(1)} collective-permute-done((f32[1,128]{1,0:T(1,128)S(1)}, f32[1,128]{1,0:T(1,128)S(1)}, u32[]{:S(2)}, u32[]{:S(2)}) %collective-permute-start.1) | collective-permute-done | bytes 544 | tf_op jit(solution)/shard_map/while/body/eval_jaxpr/ppermute | solution.py:12
  132.9 5.9 %collective-permute-done.1 = f32[1,128]{1,0:T(1,128)S(1)} collective-permute-done((f32[1,128]{1,0:T(1,128)S(1)}, f32[1,128]{1,0:T(1,128)S(1)}, u32[]{:S(2)}, u32[]{:S(2)}) %collective-permute-start.1) | collective-permute-done | bytes 544 | tf_op jit(solution)/shard_map/while/body/eval_jaxpr/ppermute | solution.py:12
  140.8 5.9 %collective-permute-done.1 = f32[1,128]{1,0:T(1,128)S(1)} collective-permute-done((f32[1,128]{1,0:T(1,128)S(1)}, f32[1,128]{1,0:T(1,128)S(1)}, u32[]{:S(2)}, u32[]{:S(2)}) %collective-permute-start.1) | collective-permute-done | bytes 544 | tf_op jit(solution)/shard_map/while/body/eval_jaxpr/ppermute | solution.py:12
  148.6 5.9 %collective-permute-done.1 = f32[1,128]{1,0:T(1,128)S(1)} collective-permute-done((f32[1,128]{1,0:T(1,128)S(1)}, f32[1,128]{1,0:T(1,128)S(1)}, u32[]{:S(2)}, u32[]{:S(2)}) %collective-permute-start.1) | collective-permute-done | bytes 544 | tf_op jit(solution)/shard_map/while/body/eval_jaxpr/ppermute | solution.py:12
  156.4 5.9 %collective-permute-done.1 = f32[1,128]{1,0:T(1,128)S(1)} collective-permute-done((f32[1,128]{1,0:T(1,128)S(1)}, f32[1,128]{1,0:T(1,128)S(1)}, u32[]{:S(2)}, u32[]{:S(2)}) %collective-permute-start.1) | collective-permute-done | bytes 544 | tf_op jit(solution)/shard_map/while/body/eval_jaxpr/ppermute | solution.py:12
  164.2 5.9 %collective-permute-done.1 = f32[1,128]{1,0:T(1,128)S(1)} collective-permute-done((f32[1,128]{1,0:T(1,128)S(1)}, f32[1,128]{1,0:T(1,128)S(1)}, u32[]{:S(2)}, u32[]{:S(2)}) %collective-permute-start.1) | collective-permute-done | bytes 544 | tf_op jit(solution)/shard_map/while/body/eval_jaxpr/ppermute | solution.py:12
  172.1 5.9 %collective-permute-done.1 = f32[1,128]{1,0:T(1,128)S(1)} collective-permute-done((f32[1,128]{1,0:T(1,128)S(1)}, f32[1,128]{1,0:T(1,128)S(1)}, u32[]{:S(2)}, u32[]{:S(2)}) %collective-permute-start.1) | collective-permute-done | bytes 544 | tf_op jit(solution)/shard_map/while/body/eval_jaxpr/ppermute | solution.py:12
  179.9 5.9 %collective-permute-done.1 = f32[1,128]{1,0:T(1,128)S(1)} collective-permute-done((f32[1,128]{1,0:T(1,128)S(1)}, f32[1,128]{1,0:T(1,128)S(1)}, u32[]{:S(2)}, u32[]{:S(2)}) %collective-permute-start.1) | collective-permute-done | bytes 544 | tf_op jit(solution)/shard_map/while/body/eval_jaxpr/ppermute | solution.py:12
  187.7 5.9 %collective-permute-done.1 = f32[1,128]{1,0:T(1,128)S(1)} collective-permute-done((f32[1,128]{1,0:T(1,128)S(1)}, f32[1,128]{1,0:T(1,128)S(1)}, u32[]{:S(2)}, u32[]{:S(2)}) %collective-permute-start.1) | collective-permute-done | bytes 544 | tf_op jit(solution)/shard_map/while/body/eval_jaxpr/ppermute | solution.py:12
  195.5 5.9 %collective-permute-done.1 = f32[1,128]{1,0:T(1,128)S(1)} collective-permute-done((f32[1,128]{1,0:T(1,128)S(1)}, f32[1,128]{1,0:T(1,128)S(1)}, u32[]{:S(2)}, u32[]{:S(2)}) %collective-permute-start.1) | collective-permute-done | bytes 544 | tf_op jit(solution)/shard_map/while/body/eval_jaxpr/ppermute | solution.py:12
  203.4 5.9 %collective-permute-done.1 = f32[1,128]{1,0:T(1,128)S(1)} collective-permute-done((f32[1,128]{1,0:T(1,128)S(1)}, f32[1,128]{1,0:T(1,128)S(1)}, u32[]{:S(2)}, u32[]{:S(2)}) %collective-permute-start.1) | collective-permute-done | bytes 544 | tf_op jit(solution)/shard_map/while/body/eval_jaxpr/ppermute | solution.py:12
  211.2 5.9 %collective-permute-done.1 = f32[1,128]{1,0:T(1,128)S(1)} collective-permute-done((f32[1,128]{1,0:T(1,128)S(1)}, f32[1,128]{1,0:T(1,128)S(1)}, u32[]{:S(2)}, u32[]{:S(2)}) %collective-permute-start.1) | collective-permute-done | bytes 544 | tf_op jit(solution)/shard_map/while/body/eval_jaxpr/ppermute | solution.py:12
  219.0 5.9 %collective-permute-done.1 = f32[1,128]{1,0:T(1,128)S(1)} collective-permute-done((f32[1,128]{1,0:T(1,128)S(1)}, f32[1,128]{1,0:T(1,128)S(1)}, u32[]{:S(2)}, u32[]{:S(2)}) %collective-permute-start.1) | collective-permute-done | bytes 544 | tf_op jit(solution)/shard_map/while/body/eval_jaxpr/ppermute | solution.py:12
  226.8 5.9 %collective-permute-done.1 = f32[1,128]{1,0:T(1,128)S(1)} collective-permute-done((f32[1,128]{1,0:T(1,128)S(1)}, f32[1,128]{1,0:T(1,128)S(1)}, u32[]{:S(2)}, u32[]{:S(2)}) %collective-permute-start.1) | collective-permute-done | bytes 544 | tf_op jit(solution)/shard_map/while/body/eval_jaxpr/ppermute | solution.py:12
  234.6 5.9 %collective-permute-done.1 = f32[1,128]{1,0:T(1,128)S(1)} collective-permute-done((f32[1,128]{1,0:T(1,128)S(1)}, f32[1,128]{1,0:T(1,128)S(1)}, u32[]{:S(2)}, u32[]{:S(2)}) %collective-permute-start.1) | collective-permute-done | bytes 544 | tf_op jit(solution)/shard_map/while/body/eval_jaxpr/ppermute | solution.py:12
  242.5 5.9 %collective-permute-done.1 = f32[1,128]{1,0:T(1,128)S(1)} collective-permute-done((f32[1,128]{1,0:T(1,128)S(1)}, f32[1,128]{1,0:T(1,128)S(1)}, u32[]{:S(2)}, u32[]{:S(2)}) %collective-permute-start.1) | collective-permute-done | bytes 544 | tf_op jit(solution)/shard_map/while/body/eval_jaxpr/ppermute | solution.py:12
  250.3 5.9 %collective-permute-done.1 = f32[1,128]{1,0:T(1,128)S(1)} collective-permute-done((f32[1,128]{1,0:T(1,128)S(1)}, f32[1,128]{1,0:T(1,128)S(1)}, u32[]{:S(2)}, u32[]{:S(2)}) %collective-permute-start.1) | collective-permute-done | bytes 544 | tf_op jit(solution)/shard_map/while/body/eval_jaxpr/ppermute | solution.py:12
  258.1 5.9 %collective-permute-done.1 = f32[1,128]{1,0:T(1,128)S(1)} collective-permute-done((f32[1,128]{1,0:T(1,128)S(1)}, f32[1,128]{1,0:T(1,128)S(1)}, u32[]{:S(2)}, u32[]{:S(2)}) %collective-permute-start.1) | collective-permute-done | bytes 544 | tf_op jit(solution)/shard_map/while/body/eval_jaxpr/ppermute | solution.py:12
  265.9 5.9 %collective-permute-done.1 = f32[1,128]{1,0:T(1,128)S(1)} collective-permute-done((f32[1,128]{1,0:T(1,128)S(1)}, f32[1,128]{1,0:T(1,128)S(1)}, u32[]{:S(2)}, u32[]{:S(2)}) %collective-permute-start.1) | collective-permute-done | bytes 544 | tf_op jit(solution)/shard_map/while/body/eval_jaxpr/ppermute | solution.py:12
  273.8 5.9 %collective-permute-done.1 = f32[1,128]{1,0:T(1,128)S(1)} collective-permute-done((f32[1,128]{1,0:T(1,128)S(1)}, f32[1,128]{1,0:T(1,128)S(1)}, u32[]{:S(2)}, u32[]{:S(2)}) %collective-permute-start.1) | collective-permute-done | bytes 544 | tf_op jit(solution)/shard_map/while/body/eval_jaxpr/ppermute | solution.py:12
  279.7 0.7 divide_convert_fusion
  (445 shorter events, 54.2 us)
Async XLA Ops:
  0.0 27.4 %all-to-all-start = ((bf16[8,1,24,16,256]{4,3,2,1,0:T(8,128)(2,1)}), bf16[8,1,24,16,256]{4,3,2,1,0:T(8,128)(2,1)S(1)}, u32[]{:S(2)}, u32[]{:S(2)}) async-start(bf16[8,1,24,16,256]{4,3,2,1,0:T(8,128)(2,1)} %bitcast.59), calls=%async_computation | async-start | bytes 3145728 | tf_op jit(solution)/shard_map/all_to_all | solution.py:67
  29.0 8.2 %collective-permute-start.3 = (f32[1,128,128]{2,1,0:T(8,128)S(1)}, f32[1,128,128]{2,1,0:T(8,128)S(1)}, u32[]{:S(2)}, u32[]{:S(2)}) collective-permute-start(f32[1,128,128]{2,1,0:T(8,128)S(1)} %fusion.30), channel_id=1, source_target_pairs={{248,0},{0,8},{8,16},{16,24},{24,32},{32,40},{40,48},{48,56},{56,6... | collective-permute-start | bytes 196616 | tf_op jit(solution)/shard_map/while/body/eval_jaxpr/ppermute | solution.py:12
  29.1 8.1 %collective-permute-start = (bf16[1,128,128]{2,1,0:T(8,128)(2,1)S(1)}, bf16[1,128,128]{2,1,0:T(8,128)(2,1)S(1)}, u32[]{:S(2)}, u32[]{:S(2)}) collective-permute-start(bf16[1,128,128]{2,1,0:T(8,128)(2,1)S(1)} %copy.10), channel_id=1, source_target_pairs={{248,0},{0,8},{8,16},{16,24},{24,32},{32,40},{40,48},{48,56},{56,6... | collective-permute-start | bytes 98312 | tf_op jit(solution)/shard_map/while/body/eval_jaxpr/ppermute | solution.py:12
  30.4 6.8 %collective-permute-start.1 = (f32[1,128]{1,0:T(1,128)S(1)}, f32[1,128]{1,0:T(1,128)S(1)}, u32[]{:S(2)}, u32[]{:S(2)}) collective-permute-start(f32[1,128]{1,0:T(1,128)S(1)} %get-tuple-element.133), channel_id=1, source_target_pairs={{248,0},{0,8},{8,16},{16,24},{24,32},{32,40},{40,48},{48,56},{56,6... | collective-permute-start | bytes 1544 | tf_op jit(solution)/shard_map/while/body/eval_jaxpr/ppermute | solution.py:12
  30.5 6.7 %collective-permute-start.2 = (f32[1,128]{1,0:T(1,128)S(1)}, f32[1,128]{1,0:T(1,128)S(1)}, u32[]{:S(2)}, u32[]{:S(2)}) collective-permute-start(f32[1,128]{1,0:T(1,128)S(1)} %get-tuple-element.134), channel_id=1, source_target_pairs={{248,0},{0,8},{8,16},{16,24},{24,32},{32,40},{40,48},{48,56},{56,6... | collective-permute-start | bytes 1544 | tf_op jit(solution)/shard_map/while/body/eval_jaxpr/ppermute | solution.py:12
  38.7 6.3 %collective-permute-start.3 = (f32[1,128,128]{2,1,0:T(8,128)S(1)}, f32[1,128,128]{2,1,0:T(8,128)S(1)}, u32[]{:S(2)}, u32[]{:S(2)}) collective-permute-start(f32[1,128,128]{2,1,0:T(8,128)S(1)} %fusion.30), channel_id=1, source_target_pairs={{248,0},{0,8},{8,16},{16,24},{24,32},{32,40},{40,48},{48,56},{56,6... | collective-permute-start | bytes 196616 | tf_op jit(solution)/shard_map/while/body/eval_jaxpr/ppermute | solution.py:12
  38.8 6.2 %collective-permute-start = (bf16[1,128,128]{2,1,0:T(8,128)(2,1)S(1)}, bf16[1,128,128]{2,1,0:T(8,128)(2,1)S(1)}, u32[]{:S(2)}, u32[]{:S(2)}) collective-permute-start(bf16[1,128,128]{2,1,0:T(8,128)(2,1)S(1)} %copy.10), channel_id=1, source_target_pairs={{248,0},{0,8},{8,16},{16,24},{24,32},{32,40},{40,48},{48,56},{56,6... | collective-permute-start | bytes 98312 | tf_op jit(solution)/shard_map/while/body/eval_jaxpr/ppermute | solution.py:12
  46.5 6.3 %collective-permute-start.3 = (f32[1,128,128]{2,1,0:T(8,128)S(1)}, f32[1,128,128]{2,1,0:T(8,128)S(1)}, u32[]{:S(2)}, u32[]{:S(2)}) collective-permute-start(f32[1,128,128]{2,1,0:T(8,128)S(1)} %fusion.30), channel_id=1, source_target_pairs={{248,0},{0,8},{8,16},{16,24},{24,32},{32,40},{40,48},{48,56},{56,6... | collective-permute-start | bytes 196616 | tf_op jit(solution)/shard_map/while/body/eval_jaxpr/ppermute | solution.py:12
  46.6 6.2 %collective-permute-start = (bf16[1,128,128]{2,1,0:T(8,128)(2,1)S(1)}, bf16[1,128,128]{2,1,0:T(8,128)(2,1)S(1)}, u32[]{:S(2)}, u32[]{:S(2)}) collective-permute-start(bf16[1,128,128]{2,1,0:T(8,128)(2,1)S(1)} %copy.10), channel_id=1, source_target_pairs={{248,0},{0,8},{8,16},{16,24},{24,32},{32,40},{40,48},{48,56},{56,6... | collective-permute-start | bytes 98312 | tf_op jit(solution)/shard_map/while/body/eval_jaxpr/ppermute | solution.py:12
  54.3 6.3 %collective-permute-start.3 = (f32[1,128,128]{2,1,0:T(8,128)S(1)}, f32[1,128,128]{2,1,0:T(8,128)S(1)}, u32[]{:S(2)}, u32[]{:S(2)}) collective-permute-start(f32[1,128,128]{2,1,0:T(8,128)S(1)} %fusion.30), channel_id=1, source_target_pairs={{248,0},{0,8},{8,16},{16,24},{24,32},{32,40},{40,48},{48,56},{56,6... | collective-permute-start | bytes 196616 | tf_op jit(solution)/shard_map/while/body/eval_jaxpr/ppermute | solution.py:12
  54.4 6.2 %collective-permute-start = (bf16[1,128,128]{2,1,0:T(8,128)(2,1)S(1)}, bf16[1,128,128]{2,1,0:T(8,128)(2,1)S(1)}, u32[]{:S(2)}, u32[]{:S(2)}) collective-permute-start(bf16[1,128,128]{2,1,0:T(8,128)(2,1)S(1)} %copy.10), channel_id=1, source_target_pairs={{248,0},{0,8},{8,16},{16,24},{24,32},{32,40},{40,48},{48,56},{56,6... | collective-permute-start | bytes 98312 | tf_op jit(solution)/shard_map/while/body/eval_jaxpr/ppermute | solution.py:12
  62.2 6.3 %collective-permute-start.3 = (f32[1,128,128]{2,1,0:T(8,128)S(1)}, f32[1,128,128]{2,1,0:T(8,128)S(1)}, u32[]{:S(2)}, u32[]{:S(2)}) collective-permute-start(f32[1,128,128]{2,1,0:T(8,128)S(1)} %fusion.30), channel_id=1, source_target_pairs={{248,0},{0,8},{8,16},{16,24},{24,32},{32,40},{40,48},{48,56},{56,6... | collective-permute-start | bytes 196616 | tf_op jit(solution)/shard_map/while/body/eval_jaxpr/ppermute | solution.py:12
  62.3 6.2 %collective-permute-start = (bf16[1,128,128]{2,1,0:T(8,128)(2,1)S(1)}, bf16[1,128,128]{2,1,0:T(8,128)(2,1)S(1)}, u32[]{:S(2)}, u32[]{:S(2)}) collective-permute-start(bf16[1,128,128]{2,1,0:T(8,128)(2,1)S(1)} %copy.10), channel_id=1, source_target_pairs={{248,0},{0,8},{8,16},{16,24},{24,32},{32,40},{40,48},{48,56},{56,6... | collective-permute-start | bytes 98312 | tf_op jit(solution)/shard_map/while/body/eval_jaxpr/ppermute | solution.py:12
  70.0 6.3 %collective-permute-start.3 = (f32[1,128,128]{2,1,0:T(8,128)S(1)}, f32[1,128,128]{2,1,0:T(8,128)S(1)}, u32[]{:S(2)}, u32[]{:S(2)}) collective-permute-start(f32[1,128,128]{2,1,0:T(8,128)S(1)} %fusion.30), channel_id=1, source_target_pairs={{248,0},{0,8},{8,16},{16,24},{24,32},{32,40},{40,48},{48,56},{56,6... | collective-permute-start | bytes 196616 | tf_op jit(solution)/shard_map/while/body/eval_jaxpr/ppermute | solution.py:12
  70.1 6.2 %collective-permute-start = (bf16[1,128,128]{2,1,0:T(8,128)(2,1)S(1)}, bf16[1,128,128]{2,1,0:T(8,128)(2,1)S(1)}, u32[]{:S(2)}, u32[]{:S(2)}) collective-permute-start(bf16[1,128,128]{2,1,0:T(8,128)(2,1)S(1)} %copy.10), channel_id=1, source_target_pairs={{248,0},{0,8},{8,16},{16,24},{24,32},{32,40},{40,48},{48,56},{56,6... | collective-permute-start | bytes 98312 | tf_op jit(solution)/shard_map/while/body/eval_jaxpr/ppermute | solution.py:12
  77.8 6.3 %collective-permute-start.3 = (f32[1,128,128]{2,1,0:T(8,128)S(1)}, f32[1,128,128]{2,1,0:T(8,128)S(1)}, u32[]{:S(2)}, u32[]{:S(2)}) collective-permute-start(f32[1,128,128]{2,1,0:T(8,128)S(1)} %fusion.30), channel_id=1, source_target_pairs={{248,0},{0,8},{8,16},{16,24},{24,32},{32,40},{40,48},{48,56},{56,6... | collective-permute-start | bytes 196616 | tf_op jit(solution)/shard_map/while/body/eval_jaxpr/ppermute | solution.py:12
  77.9 6.2 %collective-permute-start = (bf16[1,128,128]{2,1,0:T(8,128)(2,1)S(1)}, bf16[1,128,128]{2,1,0:T(8,128)(2,1)S(1)}, u32[]{:S(2)}, u32[]{:S(2)}) collective-permute-start(bf16[1,128,128]{2,1,0:T(8,128)(2,1)S(1)} %copy.10), channel_id=1, source_target_pairs={{248,0},{0,8},{8,16},{16,24},{24,32},{32,40},{40,48},{48,56},{56,6... | collective-permute-start | bytes 98312 | tf_op jit(solution)/shard_map/while/body/eval_jaxpr/ppermute | solution.py:12
  85.6 6.3 %collective-permute-start.3 = (f32[1,128,128]{2,1,0:T(8,128)S(1)}, f32[1,128,128]{2,1,0:T(8,128)S(1)}, u32[]{:S(2)}, u32[]{:S(2)}) collective-permute-start(f32[1,128,128]{2,1,0:T(8,128)S(1)} %fusion.30), channel_id=1, source_target_pairs={{248,0},{0,8},{8,16},{16,24},{24,32},{32,40},{40,48},{48,56},{56,6... | collective-permute-start | bytes 196616 | tf_op jit(solution)/shard_map/while/body/eval_jaxpr/ppermute | solution.py:12
  85.7 6.2 %collective-permute-start = (bf16[1,128,128]{2,1,0:T(8,128)(2,1)S(1)}, bf16[1,128,128]{2,1,0:T(8,128)(2,1)S(1)}, u32[]{:S(2)}, u32[]{:S(2)}) collective-permute-start(bf16[1,128,128]{2,1,0:T(8,128)(2,1)S(1)} %copy.10), channel_id=1, source_target_pairs={{248,0},{0,8},{8,16},{16,24},{24,32},{32,40},{40,48},{48,56},{56,6... | collective-permute-start | bytes 98312 | tf_op jit(solution)/shard_map/while/body/eval_jaxpr/ppermute | solution.py:12
  93.5 6.3 %collective-permute-start.3 = (f32[1,128,128]{2,1,0:T(8,128)S(1)}, f32[1,128,128]{2,1,0:T(8,128)S(1)}, u32[]{:S(2)}, u32[]{:S(2)}) collective-permute-start(f32[1,128,128]{2,1,0:T(8,128)S(1)} %fusion.30), channel_id=1, source_target_pairs={{248,0},{0,8},{8,16},{16,24},{24,32},{32,40},{40,48},{48,56},{56,6... | collective-permute-start | bytes 196616 | tf_op jit(solution)/shard_map/while/body/eval_jaxpr/ppermute | solution.py:12
  101.3 6.3 %collective-permute-start.3 = (f32[1,128,128]{2,1,0:T(8,128)S(1)}, f32[1,128,128]{2,1,0:T(8,128)S(1)}, u32[]{:S(2)}, u32[]{:S(2)}) collective-permute-start(f32[1,128,128]{2,1,0:T(8,128)S(1)} %fusion.30), channel_id=1, source_target_pairs={{248,0},{0,8},{8,16},{16,24},{24,32},{32,40},{40,48},{48,56},{56,6... | collective-permute-start | bytes 196616 | tf_op jit(solution)/shard_map/while/body/eval_jaxpr/ppermute | solution.py:12
  109.1 6.3 %collective-permute-start.3 = (f32[1,128,128]{2,1,0:T(8,128)S(1)}, f32[1,128,128]{2,1,0:T(8,128)S(1)}, u32[]{:S(2)}, u32[]{:S(2)}) collective-permute-start(f32[1,128,128]{2,1,0:T(8,128)S(1)} %fusion.30), channel_id=1, source_target_pairs={{248,0},{0,8},{8,16},{16,24},{24,32},{32,40},{40,48},{48,56},{56,6... | collective-permute-start | bytes 196616 | tf_op jit(solution)/shard_map/while/body/eval_jaxpr/ppermute | solution.py:12
  116.9 6.3 %collective-permute-start.3 = (f32[1,128,128]{2,1,0:T(8,128)S(1)}, f32[1,128,128]{2,1,0:T(8,128)S(1)}, u32[]{:S(2)}, u32[]{:S(2)}) collective-permute-start(f32[1,128,128]{2,1,0:T(8,128)S(1)} %fusion.30), channel_id=1, source_target_pairs={{248,0},{0,8},{8,16},{16,24},{24,32},{32,40},{40,48},{48,56},{56,6... | collective-permute-start | bytes 196616 | tf_op jit(solution)/shard_map/while/body/eval_jaxpr/ppermute | solution.py:12
  117.0 6.2 %collective-permute-start = (bf16[1,128,128]{2,1,0:T(8,128)(2,1)S(1)}, bf16[1,128,128]{2,1,0:T(8,128)(2,1)S(1)}, u32[]{:S(2)}, u32[]{:S(2)}) collective-permute-start(bf16[1,128,128]{2,1,0:T(8,128)(2,1)S(1)} %copy.10), channel_id=1, source_target_pairs={{248,0},{0,8},{8,16},{16,24},{24,32},{32,40},{40,48},{48,56},{56,6... | collective-permute-start | bytes 98312 | tf_op jit(solution)/shard_map/while/body/eval_jaxpr/ppermute | solution.py:12
  124.8 6.3 %collective-permute-start.3 = (f32[1,128,128]{2,1,0:T(8,128)S(1)}, f32[1,128,128]{2,1,0:T(8,128)S(1)}, u32[]{:S(2)}, u32[]{:S(2)}) collective-permute-start(f32[1,128,128]{2,1,0:T(8,128)S(1)} %fusion.30), channel_id=1, source_target_pairs={{248,0},{0,8},{8,16},{16,24},{24,32},{32,40},{40,48},{48,56},{56,6... | collective-permute-start | bytes 196616 | tf_op jit(solution)/shard_map/while/body/eval_jaxpr/ppermute | solution.py:12
  124.8 6.2 %collective-permute-start = (bf16[1,128,128]{2,1,0:T(8,128)(2,1)S(1)}, bf16[1,128,128]{2,1,0:T(8,128)(2,1)S(1)}, u32[]{:S(2)}, u32[]{:S(2)}) collective-permute-start(bf16[1,128,128]{2,1,0:T(8,128)(2,1)S(1)} %copy.10), channel_id=1, source_target_pairs={{248,0},{0,8},{8,16},{16,24},{24,32},{32,40},{40,48},{48,56},{56,6... | collective-permute-start | bytes 98312 | tf_op jit(solution)/shard_map/while/body/eval_jaxpr/ppermute | solution.py:12
  132.6 6.3 %collective-permute-start.3 = (f32[1,128,128]{2,1,0:T(8,128)S(1)}, f32[1,128,128]{2,1,0:T(8,128)S(1)}, u32[]{:S(2)}, u32[]{:S(2)}) collective-permute-start(f32[1,128,128]{2,1,0:T(8,128)S(1)} %fusion.30), channel_id=1, source_target_pairs={{248,0},{0,8},{8,16},{16,24},{24,32},{32,40},{40,48},{48,56},{56,6... | collective-permute-start | bytes 196616 | tf_op jit(solution)/shard_map/while/body/eval_jaxpr/ppermute | solution.py:12
  132.7 6.2 %collective-permute-start = (bf16[1,128,128]{2,1,0:T(8,128)(2,1)S(1)}, bf16[1,128,128]{2,1,0:T(8,128)(2,1)S(1)}, u32[]{:S(2)}, u32[]{:S(2)}) collective-permute-start(bf16[1,128,128]{2,1,0:T(8,128)(2,1)S(1)} %copy.10), channel_id=1, source_target_pairs={{248,0},{0,8},{8,16},{16,24},{24,32},{32,40},{40,48},{48,56},{56,6... | collective-permute-start | bytes 98312 | tf_op jit(solution)/shard_map/while/body/eval_jaxpr/ppermute | solution.py:12
  140.4 6.3 %collective-permute-start.3 = (f32[1,128,128]{2,1,0:T(8,128)S(1)}, f32[1,128,128]{2,1,0:T(8,128)S(1)}, u32[]{:S(2)}, u32[]{:S(2)}) collective-permute-start(f32[1,128,128]{2,1,0:T(8,128)S(1)} %fusion.30), channel_id=1, source_target_pairs={{248,0},{0,8},{8,16},{16,24},{24,32},{32,40},{40,48},{48,56},{56,6... | collective-permute-start | bytes 196616 | tf_op jit(solution)/shard_map/while/body/eval_jaxpr/ppermute | solution.py:12
  140.5 6.2 %collective-permute-start = (bf16[1,128,128]{2,1,0:T(8,128)(2,1)S(1)}, bf16[1,128,128]{2,1,0:T(8,128)(2,1)S(1)}, u32[]{:S(2)}, u32[]{:S(2)}) collective-permute-start(bf16[1,128,128]{2,1,0:T(8,128)(2,1)S(1)} %copy.10), channel_id=1, source_target_pairs={{248,0},{0,8},{8,16},{16,24},{24,32},{32,40},{40,48},{48,56},{56,6... | collective-permute-start | bytes 98312 | tf_op jit(solution)/shard_map/while/body/eval_jaxpr/ppermute | solution.py:12
  148.2 6.3 %collective-permute-start.3 = (f32[1,128,128]{2,1,0:T(8,128)S(1)}, f32[1,128,128]{2,1,0:T(8,128)S(1)}, u32[]{:S(2)}, u32[]{:S(2)}) collective-permute-start(f32[1,128,128]{2,1,0:T(8,128)S(1)} %fusion.30), channel_id=1, source_target_pairs={{248,0},{0,8},{8,16},{16,24},{24,32},{32,40},{40,48},{48,56},{56,6... | collective-permute-start | bytes 196616 | tf_op jit(solution)/shard_map/while/body/eval_jaxpr/ppermute | solution.py:12
  148.3 6.2 %collective-permute-start = (bf16[1,128,128]{2,1,0:T(8,128)(2,1)S(1)}, bf16[1,128,128]{2,1,0:T(8,128)(2,1)S(1)}, u32[]{:S(2)}, u32[]{:S(2)}) collective-permute-start(bf16[1,128,128]{2,1,0:T(8,128)(2,1)S(1)} %copy.10), channel_id=1, source_target_pairs={{248,0},{0,8},{8,16},{16,24},{24,32},{32,40},{40,48},{48,56},{56,6... | collective-permute-start | bytes 98312 | tf_op jit(solution)/shard_map/while/body/eval_jaxpr/ppermute | solution.py:12
  156.0 6.3 %collective-permute-start.3 = (f32[1,128,128]{2,1,0:T(8,128)S(1)}, f32[1,128,128]{2,1,0:T(8,128)S(1)}, u32[]{:S(2)}, u32[]{:S(2)}) collective-permute-start(f32[1,128,128]{2,1,0:T(8,128)S(1)} %fusion.30), channel_id=1, source_target_pairs={{248,0},{0,8},{8,16},{16,24},{24,32},{32,40},{40,48},{48,56},{56,6... | collective-permute-start | bytes 196616 | tf_op jit(solution)/shard_map/while/body/eval_jaxpr/ppermute | solution.py:12
  163.9 6.3 %collective-permute-start.3 = (f32[1,128,128]{2,1,0:T(8,128)S(1)}, f32[1,128,128]{2,1,0:T(8,128)S(1)}, u32[]{:S(2)}, u32[]{:S(2)}) collective-permute-start(f32[1,128,128]{2,1,0:T(8,128)S(1)} %fusion.30), channel_id=1, source_target_pairs={{248,0},{0,8},{8,16},{16,24},{24,32},{32,40},{40,48},{48,56},{56,6... | collective-permute-start | bytes 196616 | tf_op jit(solution)/shard_map/while/body/eval_jaxpr/ppermute | solution.py:12
  171.7 6.3 %collective-permute-start.3 = (f32[1,128,128]{2,1,0:T(8,128)S(1)}, f32[1,128,128]{2,1,0:T(8,128)S(1)}, u32[]{:S(2)}, u32[]{:S(2)}) collective-permute-start(f32[1,128,128]{2,1,0:T(8,128)S(1)} %fusion.30), channel_id=1, source_target_pairs={{248,0},{0,8},{8,16},{16,24},{24,32},{32,40},{40,48},{48,56},{56,6... | collective-permute-start | bytes 196616 | tf_op jit(solution)/shard_map/while/body/eval_jaxpr/ppermute | solution.py:12
  179.5 6.3 %collective-permute-start.3 = (f32[1,128,128]{2,1,0:T(8,128)S(1)}, f32[1,128,128]{2,1,0:T(8,128)S(1)}, u32[]{:S(2)}, u32[]{:S(2)}) collective-permute-start(f32[1,128,128]{2,1,0:T(8,128)S(1)} %fusion.30), channel_id=1, source_target_pairs={{248,0},{0,8},{8,16},{16,24},{24,32},{32,40},{40,48},{48,56},{56,6... | collective-permute-start | bytes 196616 | tf_op jit(solution)/shard_map/while/body/eval_jaxpr/ppermute | solution.py:12
  187.3 6.3 %collective-permute-start.3 = (f32[1,128,128]{2,1,0:T(8,128)S(1)}, f32[1,128,128]{2,1,0:T(8,128)S(1)}, u32[]{:S(2)}, u32[]{:S(2)}) collective-permute-start(f32[1,128,128]{2,1,0:T(8,128)S(1)} %fusion.30), channel_id=1, source_target_pairs={{248,0},{0,8},{8,16},{16,24},{24,32},{32,40},{40,48},{48,56},{56,6... | collective-permute-start | bytes 196616 | tf_op jit(solution)/shard_map/while/body/eval_jaxpr/ppermute | solution.py:12
  195.2 6.3 %collective-permute-start.3 = (f32[1,128,128]{2,1,0:T(8,128)S(1)}, f32[1,128,128]{2,1,0:T(8,128)S(1)}, u32[]{:S(2)}, u32[]{:S(2)}) collective-permute-start(f32[1,128,128]{2,1,0:T(8,128)S(1)} %fusion.30), channel_id=1, source_target_pairs={{248,0},{0,8},{8,16},{16,24},{24,32},{32,40},{40,48},{48,56},{56,6... | collective-permute-start | bytes 196616 | tf_op jit(solution)/shard_map/while/body/eval_jaxpr/ppermute | solution.py:12
  203.0 6.3 %collective-permute-start.3 = (f32[1,128,128]{2,1,0:T(8,128)S(1)}, f32[1,128,128]{2,1,0:T(8,128)S(1)}, u32[]{:S(2)}, u32[]{:S(2)}) collective-permute-start(f32[1,128,128]{2,1,0:T(8,128)S(1)} %fusion.30), channel_id=1, source_target_pairs={{248,0},{0,8},{8,16},{16,24},{24,32},{32,40},{40,48},{48,56},{56,6... | collective-permute-start | bytes 196616 | tf_op jit(solution)/shard_map/while/body/eval_jaxpr/ppermute | solution.py:12
  210.8 6.3 %collective-permute-start.3 = (f32[1,128,128]{2,1,0:T(8,128)S(1)}, f32[1,128,128]{2,1,0:T(8,128)S(1)}, u32[]{:S(2)}, u32[]{:S(2)}) collective-permute-start(f32[1,128,128]{2,1,0:T(8,128)S(1)} %fusion.30), channel_id=1, source_target_pairs={{248,0},{0,8},{8,16},{16,24},{24,32},{32,40},{40,48},{48,56},{56,6... | collective-permute-start | bytes 196616 | tf_op jit(solution)/shard_map/while/body/eval_jaxpr/ppermute | solution.py:12
  218.6 6.3 %collective-permute-start.3 = (f32[1,128,128]{2,1,0:T(8,128)S(1)}, f32[1,128,128]{2,1,0:T(8,128)S(1)}, u32[]{:S(2)}, u32[]{:S(2)}) collective-permute-start(f32[1,128,128]{2,1,0:T(8,128)S(1)} %fusion.30), channel_id=1, source_target_pairs={{248,0},{0,8},{8,16},{16,24},{24,32},{32,40},{40,48},{48,56},{56,6... | collective-permute-start | bytes 196616 | tf_op jit(solution)/shard_map/while/body/eval_jaxpr/ppermute | solution.py:12
  226.5 6.3 %collective-permute-start.3 = (f32[1,128,128]{2,1,0:T(8,128)S(1)}, f32[1,128,128]{2,1,0:T(8,128)S(1)}, u32[]{:S(2)}, u32[]{:S(2)}) collective-permute-start(f32[1,128,128]{2,1,0:T(8,128)S(1)} %fusion.30), channel_id=1, source_target_pairs={{248,0},{0,8},{8,16},{16,24},{24,32},{32,40},{40,48},{48,56},{56,6... | collective-permute-start | bytes 196616 | tf_op jit(solution)/shard_map/while/body/eval_jaxpr/ppermute | solution.py:12
  234.3 6.3 %collective-permute-start.3 = (f32[1,128,128]{2,1,0:T(8,128)S(1)}, f32[1,128,128]{2,1,0:T(8,128)S(1)}, u32[]{:S(2)}, u32[]{:S(2)}) collective-permute-start(f32[1,128,128]{2,1,0:T(8,128)S(1)} %fusion.30), channel_id=1, source_target_pairs={{248,0},{0,8},{8,16},{16,24},{24,32},{32,40},{40,48},{48,56},{56,6... | collective-permute-start | bytes 196616 | tf_op jit(solution)/shard_map/while/body/eval_jaxpr/ppermute | solution.py:12
  242.1 6.3 %collective-permute-start.3 = (f32[1,128,128]{2,1,0:T(8,128)S(1)}, f32[1,128,128]{2,1,0:T(8,128)S(1)}, u32[]{:S(2)}, u32[]{:S(2)}) collective-permute-start(f32[1,128,128]{2,1,0:T(8,128)S(1)} %fusion.30), channel_id=1, source_target_pairs={{248,0},{0,8},{8,16},{16,24},{24,32},{32,40},{40,48},{48,56},{56,6... | collective-permute-start | bytes 196616 | tf_op jit(solution)/shard_map/while/body/eval_jaxpr/ppermute | solution.py:12
  249.9 6.3 %collective-permute-start.3 = (f32[1,128,128]{2,1,0:T(8,128)S(1)}, f32[1,128,128]{2,1,0:T(8,128)S(1)}, u32[]{:S(2)}, u32[]{:S(2)}) collective-permute-start(f32[1,128,128]{2,1,0:T(8,128)S(1)} %fusion.30), channel_id=1, source_target_pairs={{248,0},{0,8},{8,16},{16,24},{24,32},{32,40},{40,48},{48,56},{56,6... | collective-permute-start | bytes 196616 | tf_op jit(solution)/shard_map/while/body/eval_jaxpr/ppermute | solution.py:12
  257.7 6.3 %collective-permute-start.3 = (f32[1,128,128]{2,1,0:T(8,128)S(1)}, f32[1,128,128]{2,1,0:T(8,128)S(1)}, u32[]{:S(2)}, u32[]{:S(2)}) collective-permute-start(f32[1,128,128]{2,1,0:T(8,128)S(1)} %fusion.30), channel_id=1, source_target_pairs={{248,0},{0,8},{8,16},{16,24},{24,32},{32,40},{40,48},{48,56},{56,6... | collective-permute-start | bytes 196616 | tf_op jit(solution)/shard_map/while/body/eval_jaxpr/ppermute | solution.py:12
  265.6 6.3 %collective-permute-start.3 = (f32[1,128,128]{2,1,0:T(8,128)S(1)}, f32[1,128,128]{2,1,0:T(8,128)S(1)}, u32[]{:S(2)}, u32[]{:S(2)}) collective-permute-start(f32[1,128,128]{2,1,0:T(8,128)S(1)} %fusion.30), channel_id=1, source_target_pairs={{248,0},{0,8},{8,16},{16,24},{24,32},{32,40},{40,48},{48,56},{56,6... | collective-permute-start | bytes 196616 | tf_op jit(solution)/shard_map/while/body/eval_jaxpr/ppermute | solution.py:12
  273.4 6.3 %collective-permute-start.3 = (f32[1,128,128]{2,1,0:T(8,128)S(1)}, f32[1,128,128]{2,1,0:T(8,128)S(1)}, u32[]{:S(2)}, u32[]{:S(2)}) collective-permute-start(f32[1,128,128]{2,1,0:T(8,128)S(1)} %fusion.30), channel_id=1, source_target_pairs={{248,0},{0,8},{8,16},{16,24},{24,32},{32,40},{40,48},{48,56},{56,6... | collective-permute-start | bytes 196616 | tf_op jit(solution)/shard_map/while/body/eval_jaxpr/ppermute | solution.py:12
  (83 other events, 529.0 us)
where the time goes:
time: 281 us; the launch traced here: 280 us
  waiting for transfers between devices  208 us (74%)
  matrix products  28.4 us (10%)
  starting transfers between devices  22 us (8%)
  other arithmetic  13.3 us (5%)
  local copies, waits for them, and re-layouts  6.47 us (2%)
    ppermute x128, waiting for transfers between devices, shifted(): return lax.ppermute(block, axis, route)  188 us
    all_to_all x1, waiting for transfers between devices, body(): lax.all_to_all(grouped, 'pool', split_axis=0, concat_axis=2, tiled=True)  19.7 us
    dot_general x32, matrix products, slice_attend(): jnp.einsum('hun,hwn->huw', query_matrix, common_prefix[:, :, :head_extent...  14.5 us
    ppermute x128, starting transfers between devices, shifted(): return lax.ppermute(block, axis, route)  14.5 us
    dot_general x32, matrix products, slice_attend(): jnp.einsum('bzv,bvn->bzn', softmax_weights, common_prefix[:, :, head_exte...  13.9 us
    reduce_sum x32, other arithmetic, slice_attend(): totals = jnp.sum(exponent, axis=-1)  12.1 us
    all_to_all x1, starting transfers between devices, body(): lax.all_to_all(grouped, 'pool', split_axis=0, concat_axis=2, tiled=True)  7.57 us
  transfers between devices with their start and end apart: 129, of which 33 were waited for; matrix products, arithmetic and copies ran while one was open for 0% of the time, Pallas kernels for 0%

commit v1 on v0

v1 whole, which is shorter than its diff:
```python
import functools
import math

import jax
import jax.numpy as jnp
from jax import lax
from jax.experimental import pallas as pl
from jax.experimental.pallas import tpu as pltpu
from jax.sharding import PartitionSpec as P

MESH = pl.DeviceIdType.MESH
NZ, NX, NC = 8, 2, 2
NH, NY = 2, 4
POOL = NH * NY
BS, D = 16, 128
NB, CAP = 96, 24
ROWS = 128
SPLIT = (8, 8, 8)
PEERS = ((0, 1), (0, 3), (1, 0), (0, 2), (1, 1), (1, 3), (1, 2))
PAIR = 2 * NX * ROWS
TILES = NZ // 2
PACK = D + 16
SCALE = math.log2(math.e) / math.sqrt(D)
LOG2E = math.log2(math.e)


def slot_of(dz):
    return 0 if dz == 0 else (2 * dz - 1 if dz <= NZ // 2 else 2 * (NZ - dz))


def step_of(slot):
    return (slot + 1) // 2 if slot % 2 else (NZ - slot // 2) % NZ


def packing(owner_ref, table_ref):
    owner = owner_ref[...]
    counts = [jnp.sum((owner == j).astype(jnp.int32), axis=1, keepdims=True) for j in range(POOL)]
    place = lax.broadcasted_iota(jnp.int32, (1, 128), 1)
    source = place
    ahead = None
    start = 0
    for size in SPLIT:
        for j in range(POOL):
            here = jnp.clip(counts[j] - start, 0, size)
            ahead = here if ahead is None else ahead + here
            source = source + jnp.where(place >= ahead, size - here, 0)
        start += size
    table_ref[...] = jnp.where(place < NB, jnp.minimum(source, POOL * CAP - 1), 0)


def kernel(
    q_ref, kv_ref, owner_ref, o_ref,
    qbuf, arrived, staged, packed, table_v, table_s, vt, scores, acc, peak, total,
    xsend, xrecv, zsend, zrecv,
    kv_ssem, kv_rsem, own_sem, table_sem, qx_ssem, qx_rsem, qz_ssem, qz_rsem, c_ssem, c_rsem,
    xs_sem, xr_sem, zs_sem, zr_sem,
):
    blk, pool = lax.axis_index("blk"), lax.axis_index("pool")
    z, xl, core = blk // (NX * NC), (blk // NC) % NX, blk % NC
    xh, y = pool // NY, pool % NY

    def pool_peer(dx, dy):
        return (blk, ((xh + dx) % NH) * NY + (y + dy) % NY)

    def z_peer(dz):
        return (((z + dz) % NZ) * (NX * NC) + xl * NC + core, pool)

    x_peer = (z * (NX * NC) + (1 - xl) * NC + core, pool)
    core_peer = (z * (NX * NC) + xl * NC + (1 - core), pool)

    def remote(src, dst, ssem, rsem, device):
        return pltpu.make_async_remote_copy(
            src_ref=src, dst_ref=dst, send_sem=ssem, recv_sem=rsem, device_id=device, device_id_type=MESH
        )

    barrier = pltpu.get_barrier_semaphore()
    everyone = [z_peer(d) for d in range(1, NZ)] + [pool_peer(*p) for p in PEERS] + [x_peer, core_peer]
    for device in everyone:
        pl.semaphore_signal(barrier, inc=1, device_id=device, device_id_type=MESH)

    own = []
    start = 0
    for m, size in enumerate(SPLIT):
        copy = pltpu.make_async_copy(
            kv_ref.at[pool, pl.ds(start, size)], arrived.at[pl.ds(start * POOL + pool * size, size)], own_sem.at[m]
        )
        copy.start()
        own.append(copy)
        start += size
    qbuf[0, 0] = q_ref[...].reshape(ROWS, D)
    packing(owner_ref, table_v)
    to_smem = pltpu.make_async_copy(table_v, table_s, table_sem)
    to_smem.start()
    to_smem.wait()

    pl.semaphore_wait(barrier, len(everyone))

    qx = remote(qbuf.at[0, 0], qbuf.at[0, 1], qx_ssem, qx_rsem, x_peer)
    qx.start()
    qz = [None] * (2 * NZ)
    order = [step_of(s) for s in range(1, NZ)]
    for d in order:
        at = slot_of(NZ - d)
        qz[2 * at] = remote(qbuf.at[0, 0], qbuf.at[at, 0], qz_ssem.at[2 * at], qz_rsem.at[2 * at], z_peer(d))
        qz[2 * at].start()
    moves = []
    start = 0
    for m, size in enumerate(SPLIT):
        part = []
        for i, (dx, dy) in enumerate(PEERS):
            device = pool_peer(dx, dy)
            copy = remote(
                kv_ref.at[device[1], pl.ds(start, size)], arrived.at[pl.ds(start * POOL + pool * size, size)],
                kv_ssem.at[m, i], kv_rsem.at[m, i], device,
            )
            copy.start()
            part.append(copy)
        moves.append(part)
        start += size
        if m == 0:
            qx.wait_recv()
            for d in order:
                at = slot_of(NZ - d)
                qz[2 * at + 1] = remote(
                    qbuf.at[0, 1], qbuf.at[at, 1], qz_ssem.at[2 * at + 1], qz_rsem.at[2 * at + 1], z_peer(d)
                )
                qz[2 * at + 1].start()

    x_moves, z_moves = [None] * NZ, [None] * NZ

    def split3(v):
        high = v.astype(jnp.bfloat16)
        rest = v - high.astype(jnp.float32)
        mid = rest.astype(jnp.bfloat16)
        low = (rest - mid.astype(jnp.float32)).astype(jnp.bfloat16)
        return high, mid, low

    def put(ref, s, value, lse):
        ref[s, pl.ds(0, D)] = value.astype(jnp.bfloat16)
        parts = jnp.concatenate([p.astype(jnp.float32) for p in split3(lse)] + [jnp.zeros((13, ROWS), jnp.float32)], axis=0)
        ref[s, pl.ds(D, 16)] = parts.astype(jnp.bfloat16)

    def get(ref, s):
        tail = ref[s, pl.ds(D, 16)].astype(jnp.float32)
        return ref[s, pl.ds(0, D)].astype(jnp.float32), tail[0:1] + tail[1:2] + tail[2:3]

    def combine(s):
        x_moves[s].wait_recv()
        t, lanes = s // 2, pl.ds((s % 2) * NX * ROWS, ROWS)
        mine, lse_a = acc[t, :, lanes], peak[t, :, lanes]
        theirs, lse_b = get(xrecv, s)
        top = jnp.maximum(lse_a, lse_b)
        wa, wb = jnp.exp2(lse_a - top), jnp.exp2(lse_b - top)
        norm = wa + wb
        inv = 1.0 / norm
        put(zsend, s, mine * (wa * inv) + theirs * (wb * inv), top + jnp.log(norm) * LOG2E)
        if s > 0:
            z_moves[s] = remote(zsend.at[s], zrecv.at[s], zs_sem.at[s], zr_sem.at[s], z_peer(step_of(s)))
            z_moves[s].start()

    swaps = []
    start = 0
    last = len(SPLIT) - 1
    for m, size in enumerate(SPLIT):
        blocks = size * POOL // 2
        own[m].wait()
        for copy in moves[m]:
            copy.wait_recv()
        staged[pl.ds(start * POOL, size * POOL)] = arrived[pl.ds(start * POOL, size * POOL)]
        base = start * POOL
        for p in range(blocks):
            packed[base + p] = staged[table_s[0, start * POOL // 2 + p]]
        swap = remote(
            packed.at[pl.ds(base, blocks)], packed.at[pl.ds(base + blocks, blocks)], c_ssem.at[m], c_rsem.at[m], core_peer
        )
        swap.start()
        swaps.append(swap)
        swap.wait_recv()
        tokens = 2 * blocks * BS
        vt[m % 2, :, pl.ds(0, tokens)] = jnp.swapaxes(
            packed[pl.ds(base, 2 * blocks), :, D:].reshape(tokens, D), 0, 1
        )

        def score(t, b):
            if m == 0:
                for s in (2 * t, 2 * t + 1):
                    if s > 0:
                        qz[2 * s].wait_recv()
                        qz[2 * s + 1].wait_recv()
            keys = packed[pl.ds(base, 2 * blocks), :, :D].reshape(tokens, D)
            rows = qbuf[pl.ds(2 * t, 2)].reshape(PAIR, D)
            scores[b, pl.ds(0, tokens)] = lax.dot_general(
                keys, rows, (((1,), (1,)), ((), ())), preferred_element_type=jnp.float32
            )

        def soft(t, b):
            s = scores[b, pl.ds(0, tokens)]
            high = jnp.max(s, axis=0, keepdims=True)
            if m > 0:
                before = peak[t]
                high = jnp.maximum(high, before)
            high_c = high * SCALE
            weight = jnp.exp2(s * SCALE - high_c)
            mass = jnp.sum(weight, axis=0, keepdims=True)
            out = jnp.dot(vt[m % 2, :, pl.ds(0, tokens)], weight.astype(jnp.bfloat16), preferred_element_type=jnp.float32)
            if m > 0:
                keep = jnp.exp2(before * SCALE - high_c)
                mass = mass + keep * total[t]
                out = out + keep * acc[t]
            if m < last:
                peak[t] = high
                total[t] = mass
                acc[t] = out
                return
            out = out * (1.0 / mass)
            lse = high_c + jnp.log(mass) * LOG2E
            acc[t] = out
            peak[t] = lse
            for h in (1, 0):
                slot = 2 * t + h
                lanes = slice((2 * h + 1) * ROWS, (2 * h + 2) * ROWS)
                put(xsend, slot, out[:, lanes], lse[:, lanes])
                x_moves[slot] = remote(xsend.at[slot], xrecv.at[slot], xs_sem.at[slot], xr_sem.at[slot], x_peer)
                x_moves[slot].start()

        tiles = list(range(TILES))
        if m == last:
            tiles = tiles[::-1]
        score(tiles[0], 0)
        for i, t in enumerate(tiles):
            if i + 1 < TILES:
                score(tiles[i + 1], (i + 1) % 2)
            soft(t, i % 2)
            if m == last and i >= 1:
                combine(2 * tiles[i - 1] + 1)
                combine(2 * tiles[i - 1])
        start += size
    combine(1)
    combine(0)

    values, logs = [], []
    for s in range(NZ):
        if s > 0:
            z_moves[s].wait_recv()
        value, lse = get(zsend if s == 0 else zrecv, s)
        values.append(value)
        logs.append(lse)
    top = functools.reduce(jnp.maximum, logs)
    weights = [jnp.exp2(v - top) for v in logs]
    inv = 1.0 / functools.reduce(jnp.add, weights)
    result = functools.reduce(jnp.add, [v * (w * inv) for v, w in zip(values, weights)])
    o_ref[...] = jnp.swapaxes(result, 0, 1).astype(jnp.bfloat16).reshape(o_ref.shape)

    qx.wait_send()
    for copy in qz[2:]:
        copy.wait_send()
    for part in moves:
        for copy in part:
            copy.wait_send()
    for copy in swaps + x_moves + z_moves[1:]:
        copy.wait_send()


def body(queries, kv_cache, block_owner):
    widest = max(SPLIT) * POOL * BS
    dma = pltpu.SemaphoreType.DMA
    return pl.pallas_call(
        kernel,
        out_shape=jax.ShapeDtypeStruct(queries.shape, queries.dtype),
        in_specs=[
            pl.BlockSpec(memory_space=pltpu.VMEM),
            pl.BlockSpec(memory_space=pltpu.HBM),
            pl.BlockSpec(memory_space=pltpu.VMEM),
        ],
        out_specs=pl.BlockSpec(memory_space=pltpu.VMEM),
        scratch_shapes=[
            pltpu.VMEM((NZ, NX, ROWS, D), jnp.bfloat16),
            pltpu.VMEM((POOL * CAP, BS, 2 * D), jnp.bfloat16),
            pltpu.VMEM((POOL * CAP, BS, 2 * D), jnp.bfloat16),
            pltpu.VMEM((2 * NB, BS, 2 * D), jnp.bfloat16),
            pltpu.VMEM((1, 128), jnp.int32),
            pltpu.SMEM((1, 128), jnp.int32),
            pltpu.VMEM((2, D, widest), jnp.bfloat16),
            pltpu.VMEM((2, widest, PAIR), jnp.float32),
            pltpu.VMEM((TILES, D, PAIR), jnp.float32),
            pltpu.VMEM((TILES, 1, PAIR), jnp.float32),
            pltpu.VMEM((TILES, 1, PAIR), jnp.float32),
            pltpu.VMEM((NZ, PACK, ROWS), jnp.bfloat16),
            pltpu.VMEM((NZ, PACK, ROWS), jnp.bfloat16),
            pltpu.VMEM((NZ, PACK, ROWS), jnp.bfloat16),
            pltpu.VMEM((NZ, PACK, ROWS), jnp.bfloat16),
            dma((len(SPLIT), len(PEERS))),
            dma((len(SPLIT), len(PEERS))),
            dma((len(SPLIT),)),
            dma,
            dma,
            dma,
            dma((2 * NZ,)),
            dma((2 * NZ,)),
            dma((len(SPLIT),)),
            dma((len(SPLIT),)),
            dma((NZ,)),
            dma((NZ,)),
            dma((NZ,)),
            dma((NZ,)),
        ],
        compiler_params=pltpu.CompilerParams(
            collective_id=0, has_side_effects=True, vmem_limit_bytes=48 * 1024 * 1024
        ),
        cost_estimate=pl.CostEstimate(flops=3_300_000_000, bytes_accessed=4_000_000, transcendentals=6_300_000),
    )(queries, kv_cache, block_owner.reshape(1, NB))


def solution(mesh):
    in_specs = (P("blk", "pool", None), P(None, ("blk", "pool"), None, None), P("blk", None))
    out_specs = P("blk", "pool", None)
    return jax.shard_map(body, mesh=mesh, in_specs=in_specs, out_specs=out_specs, check_vma=False)
```

time: 281 us -> 49.7 us (0.18)
  waiting for transfers between devices: 208 us -> 0 us
  Pallas kernels: 0 us -> 46.1 us
  matrix products: 28.4 us -> 0 us
  starting transfers between devices: 22 us -> 0 us
  other arithmetic: 13.3 us -> 0 us
  local copies, waits for them, and re-layouts: 6.47 us -> 3.44 us
    ppermute x128 -> x0, waiting for transfers between devices: 188 us -> none  [shifted(): return lax.ppermute(block, axis, route)]
    pallas_call x0 -> x1, Pallas kernels: none -> 46.1 us  [body(): pl.pallas_call(kernel, out_shape=jax.ShapeDtypeStruct(queries.shape, quer...]
    dot_general x64 -> x0, matrix products: 28.4 us -> none  [the longest x32 14.5 us: slice_attend(): jnp.einsum('hun,hwn->huw', query_matrix, common_prefix[:, :, :head_extent...]
    all_to_all x1 -> x0, waiting for transfers between devices: 19.7 us -> none  [body(): lax.all_to_all(grouped, 'pool', split_axis=0, concat_axis=2, tiled=True)]
    ppermute x128 -> x0, starting transfers between devices: 14.5 us -> none  [shifted(): return lax.ppermute(block, axis, route)]
    reduce_sum x33 -> x0, other arithmetic: 12.2 us -> none  [the longest x32 12.1 us: slice_attend(): totals = jnp.sum(exponent, axis=-1)]
    all_to_all x1 -> x0, starting transfers between devices: 7.57 us -> none  [body(): lax.all_to_all(grouped, 'pool', split_axis=0, concat_axis=2, tiled=True)]
    broadcast_in_dim x67 -> x0, local copies, waits for them, and re-layouts: 6.32 us -> none  [the longest x32 3.47 us: slice_attend(): jnp.where(valid_tokens[None, None, :], attention_logits, -1e+30)]
  transfers between devices with their start and end apart: 129 -> 0, of which waited for: 33 -> 0; matrix products, arithmetic and copies ran while one was open for 0% -> 0% of each run, Pallas kernels for 0% -> 0%
where the time goes in v1:
time: 49.7 us; the launch traced here: 49.5 us
  Pallas kernels  46.1 us (93%)
  local copies, waits for them, and re-layouts  3.44 us (7%)
    pallas_call x1, Pallas kernels, body(): pl.pallas_call(kernel, out_shape=jax.ShapeDtypeStruct(queries.shape, quer...  46.1 us
    unnamed x7, local copies, waits for them, and re-layouts  3.44 us

profile of v1, /device:TPU:4, one launch (start us, length us, event | category | flops | bytes accessed | tf_op | source)
XLA Modules:
  0.0 49.5 jit_solution(15142936554443349896)
XLA Ops:
  0.0 0.0 copy-start
  0.0 1.4 %copy-done = bf16[8,24,16,256]{3,2,1,0:T(8,128)(2,1)S(1)} copy-done((bf16[8,24,16,256]{3,2,1,0:T(8,128)(2,1)S(1)}, bf16[8,24,16,256]{3,2,1,0:T(8,128)(2,1)}, u32[]{:S(2)}) %copy-start) | copy-done | bytes 1572888
  1.4 0.0 copy-start.1
  1.4 0.8 %copy-done.1 = bf16[8,16,128]{2,1,0:T(8,128)(2,1)S(1)} copy-done((bf16[8,16,128]{2,1,0:T(8,128)(2,1)S(1)}, bf16[8,16,128]{2,1,0:T(8,128)(2,1)}, u32[]{:S(2)}) %copy-start.1) | copy-done | bytes 32792
  2.2 0.0 copy-start.2
  2.2 0.7 %copy-done.2 = s32[96,1]{0,1:T(1,128)S(1)} copy-done((s32[96,1]{0,1:T(1,128)S(1)}, s32[96,1]{0,1:T(1,128)}, u32[]{:S(2)}) %copy-start.2) | copy-done | bytes 408
  2.8 46.1 %shard_map.37 = bf16[8,16,128]{2,1,0:T(8,128)(2,1)S(1)} custom-call(bf16[8,16,128]{2,1,0:T(8,128)(2,1)S(1)} %copy-done.1, bf16[8,24,16,256]{3,2,1,0:T(8,128)(2,1)S(1)} %copy-done, s32[1,96]{1,0:T(1,128)S(1)} %bitcast.1), custom_call_target="tpu_custom_call" | custom-call | flops 3300000000 | bytes 4000000 | tf_op jit(solution)/shard_map/pallas_call | solution.py:267
  48.9 0.6 %copy.5 = bf16[8,16,128]{2,1,0:T(8,128)(2,1)} copy(bf16[8,16,128]{2,1,0:T(8,128)(2,1)S(1)} %shard_map.37) | data formatting | bytes 65536
Async XLA Ops:
  0.0 1.4 %copy-start = (bf16[8,24,16,256]{3,2,1,0:T(8,128)(2,1)S(1)}, bf16[8,24,16,256]{3,2,1,0:T(8,128)(2,1)}, u32[]{:S(2)}) copy-start(bf16[8,24,16,256]{3,2,1,0:T(8,128)(2,1)} %kv_ref.1) | copy-start | bytes 4718596
  1.4 0.8 %copy-start.1 = (bf16[8,16,128]{2,1,0:T(8,128)(2,1)S(1)}, bf16[8,16,128]{2,1,0:T(8,128)(2,1)}, u32[]{:S(2)}) copy-start(bf16[8,16,128]{2,1,0:T(8,128)(2,1)} %q_ref.1) | copy-start | bytes 98308
  2.2 0.7 %copy-start.2 = (s32[96,1]{0,1:T(1,128)S(1)}, s32[96,1]{0,1:T(1,128)}, u32[]{:S(2)}) copy-start(s32[96,1]{0,1:T(1,128)} %param.5) | copy-start | bytes 1156

commit v2 on v1

--- a/solution.py
+++ b/solution.py
@@ -14,9 +14,10 @@
 POOL = NH * NY
 BS, D = 16, 128
 NB, CAP = 96, 24
-ROWS = 128
+REQ, HEADS = 8, 16
+ROWS = REQ * HEADS
 SPLIT = (8, 8, 8)
-PEERS = ((0, 1), (0, 3), (1, 0), (0, 2), (1, 1), (1, 3), (1, 2))
+PEERS = ((1, 2), (1, 1), (1, 3), (1, 0), (0, 2), (0, 1), (0, 3))
 PAIR = 2 * NX * ROWS
 TILES = NZ // 2
 PACK = D + 16
@@ -50,9 +51,9 @@
 
 def kernel(
     q_ref, kv_ref, owner_ref, o_ref,
-    qbuf, arrived, staged, packed, table_v, table_s, vt, scores, acc, peak, total,
+    owner_v, kv_v, qbuf, arrived, staged, packed, table_v, table_s, vt, scores, acc, peak, total,
     xsend, xrecv, zsend, zrecv,
-    kv_ssem, kv_rsem, own_sem, table_sem, qx_ssem, qx_rsem, qz_ssem, qz_rsem, c_ssem, c_rsem,
+    kv_ssem, kv_rsem, own_sem, first_sem, table_sem, qx_ssem, qx_rsem, qz_ssem, qz_rsem, c_ssem, c_rsem,
     xs_sem, xr_sem, zs_sem, zr_sem,
 ):
     blk, pool = lax.axis_index("blk"), lax.axis_index("pool")
@@ -78,39 +79,41 @@
     for device in everyone:
         pl.semaphore_signal(barrier, inc=1, device_id=device, device_id_type=MESH)
 
-    own = []
+    rows_in = pltpu.make_async_copy(q_ref, qbuf.at[0, 0], first_sem.at[0])
+    rows_in.start()
+    owners_in = pltpu.make_async_copy(owner_ref, owner_v, first_sem.at[1])
+    owners_in.start()
+    held = []
     start = 0
     for m, size in enumerate(SPLIT):
-        copy = pltpu.make_async_copy(
-            kv_ref.at[pool, pl.ds(start, size)], arrived.at[pl.ds(start * POOL + pool * size, size)], own_sem.at[m]
-        )
+        copy = pltpu.make_async_copy(kv_ref.at[:, pl.ds(start, size)], kv_v.at[:, pl.ds(start, size)], own_sem.at[m])
         copy.start()
-        own.append(copy)
+        held.append(copy)
         start += size
-    qbuf[0, 0] = q_ref[...].reshape(ROWS, D)
-    packing(owner_ref, table_v)
-    to_smem = pltpu.make_async_copy(table_v, table_s, table_sem)
-    to_smem.start()
-    to_smem.wait()
-
+    rows_in.wait()
     pl.semaphore_wait(barrier, len(everyone))
 
     qx = remote(qbuf.at[0, 0], qbuf.at[0, 1], qx_ssem, qx_rsem, x_peer)
     qx.start()
     qz = [None] * (2 * NZ)
     order = [step_of(s) for s in range(1, NZ)]
-    for d in order:
-        at = slot_of(NZ - d)
-        qz[2 * at] = remote(qbuf.at[0, 0], qbuf.at[at, 0], qz_ssem.at[2 * at], qz_rsem.at[2 * at], z_peer(d))
-        qz[2 * at].start()
+
+    def send_rows(h):
+        for d in order:
+            at = slot_of(NZ - d)
+            k = 2 * at + h
+            qz[k] = remote(qbuf.at[0, h], qbuf.at[at, h], qz_ssem.at[k], qz_rsem.at[k], z_peer(d))
+            qz[k].start()
+
     moves = []
     start = 0
     for m, size in enumerate(SPLIT):
+        held[m].wait()
         part = []
         for i, (dx, dy) in enumerate(PEERS):
             device = pool_peer(dx, dy)
             copy = remote(
-                kv_ref.at[device[1], pl.ds(start, size)], arrived.at[pl.ds(start * POOL + pool * size, size)],
+                kv_v.at[device[1], pl.ds(start, size)], arrived.at[pl.ds(start * POOL + pool * size, size)],
                 kv_ssem.at[m, i], kv_rsem.at[m, i], device,
             )
             copy.start()
@@ -118,13 +121,14 @@
         moves.append(part)
         start += size
         if m == 0:
-            qx.wait_recv()
-            for d in order:
-                at = slot_of(NZ - d)
-                qz[2 * at + 1] = remote(
-                    qbuf.at[0, 1], qbuf.at[at, 1], qz_ssem.at[2 * at + 1], qz_rsem.at[2 * at + 1], z_peer(d)
-                )
-                qz[2 * at + 1].start()
+            send_rows(0)
+    qx.wait_recv()
+    send_rows(1)
+    owners_in.wait()
+    packing(owner_v, table_v)
+    to_smem = pltpu.make_async_copy(table_v, table_s, table_sem)
+    to_smem.start()
+    to_smem.wait()
 
     x_moves, z_moves = [None] * NZ, [None] * NZ
 
@@ -158,36 +162,19 @@
             z_moves[s] = remote(zsend.at[s], zrecv.at[s], zs_sem.at[s], zr_sem.at[s], z_peer(step_of(s)))
             z_moves[s].start()
 
-    swaps = []
-    start = 0
-    last = len(SPLIT) - 1
-    for m, size in enumerate(SPLIT):
-        blocks = size * POOL // 2
-        own[m].wait()
-        for copy in moves[m]:
-            copy.wait_recv()
-        staged[pl.ds(start * POOL, size * POOL)] = arrived[pl.ds(start * POOL, size * POOL)]
-        base = start * POOL
-        for p in range(blocks):
-            packed[base + p] = staged[table_s[0, start * POOL // 2 + p]]
-        swap = remote(
-            packed.at[pl.ds(base, blocks)], packed.at[pl.ds(base + blocks, blocks)], c_ssem.at[m], c_rsem.at[m], core_peer
-        )
-        swap.start()
-        swaps.append(swap)
-        swap.wait_recv()
-        tokens = 2 * blocks * BS
-        vt[m % 2, :, pl.ds(0, tokens)] = jnp.swapaxes(
-            packed[pl.ds(base, 2 * blocks), :, D:].reshape(tokens, D), 0, 1
-        )
+    def attend(turn, base, blocks, final=False):
+        first = turn == 0
+        tokens = blocks * BS
+        side = turn % 2
+        vt[side, :, pl.ds(0, tokens)] = jnp.swapaxes(packed[pl.ds(base, blocks), :, D:].reshape(tokens, D), 0, 1)
 
         def score(t, b):
-            if m == 0:
+            if first:
                 for s in (2 * t, 2 * t + 1):
                     if s > 0:
                         qz[2 * s].wait_recv()
                         qz[2 * s + 1].wait_recv()
-            keys = packed[pl.ds(base, 2 * blocks), :, :D].reshape(tokens, D)
+            keys = packed[pl.ds(base, blocks), :, :D].reshape(tokens, D)
             rows = qbuf[pl.ds(2 * t, 2)].reshape(PAIR, D)
             scores[b, pl.ds(0, tokens)] = lax.dot_general(
                 keys, rows, (((1,), (1,)), ((), ())), preferred_element_type=jnp.float32
@@ -196,18 +183,18 @@
         def soft(t, b):
             s = scores[b, pl.ds(0, tokens)]
             high = jnp.max(s, axis=0, keepdims=True)
-            if m > 0:
-                before = peak[t]
-                high = jnp.maximum(high, before)
+            if not first:
+                previous = peak[t]
+                high = jnp.maximum(high, previous)
             high_c = high * SCALE
             weight = jnp.exp2(s * SCALE - high_c)
             mass = jnp.sum(weight, axis=0, keepdims=True)
-            out = jnp.dot(vt[m % 2, :, pl.ds(0, tokens)], weight.astype(jnp.bfloat16), preferred_element_type=jnp.float32)
-            if m > 0:
-                keep = jnp.exp2(before * SCALE - high_c)
+            out = jnp.dot(vt[side, :, pl.ds(0, tokens)], weight.astype(jnp.bfloat16), preferred_element_type=jnp.float32)
+            if not first:
+                keep = jnp.exp2(previous * SCALE - high_c)
                 mass = mass + keep * total[t]
                 out = out + keep * acc[t]
-            if m < last:
+            if not final:
                 peak[t] = high
                 total[t] = mass
                 acc[t] = out
@@ -224,17 +211,42 @@
                 x_moves[slot].start()
 
         tiles = list(range(TILES))
-        if m == last:
+        if final:
             tiles = tiles[::-1]
         score(tiles[0], 0)
         for i, t in enumerate(tiles):
             if i + 1 < TILES:
                 score(tiles[i + 1], (i + 1) % 2)
             soft(t, i % 2)
-            if m == last and i >= 1:
+            if final and i >= 1:
                 combine(2 * tiles[i - 1] + 1)
                 combine(2 * tiles[i - 1])
+
+    swaps = []
+    start = 0
+    for m, size in enumerate(SPLIT):
+        blocks = size * POOL // 2
+        for copy in moves[m]:
+            copy.wait_recv()
+        staged[pl.ds(start * POOL, size * POOL)] = arrived[pl.ds(start * POOL, size * POOL)]
+        staged[pl.ds(start * POOL + pool * size, size)] = kv_v[pool, pl.ds(start, size)]
+        base = start * POOL
+        for p in range(blocks):
+            packed[base + p] = staged[table_s[0, start * POOL // 2 + p]]
+        swap = remote(
+            packed.at[pl.ds(base, blocks)], packed.at[pl.ds(base + blocks, blocks)], c_ssem.at[m], c_rsem.at[m], core_peer
+        )
+        swap.start()
+        swaps.append(swap)
+        if m == 0:
+            attend(0, 0, blocks)
+        else:
+            swaps[m - 1].wait_recv()
+            attend(m, base - before, before + blocks)
+        before = blocks
         start += size
+    swaps[-1].wait_recv()
+    attend(len(SPLIT), base + blocks, blocks, final=True)
     combine(1)
     combine(0)
 
@@ -262,19 +274,21 @@
 
 
 def body(queries, kv_cache, block_owner):
-    widest = max(SPLIT) * POOL * BS
+    widest = max(a + b for a, b in zip(SPLIT, SPLIT[1:])) * POOL // 2 * BS
     dma = pltpu.SemaphoreType.DMA
     return pl.pallas_call(
         kernel,
         out_shape=jax.ShapeDtypeStruct(queries.shape, queries.dtype),
         in_specs=[
-            pl.BlockSpec(memory_space=pltpu.VMEM),
             pl.BlockSpec(memory_space=pltpu.HBM),
-            pl.BlockSpec(memory_space=pltpu.VMEM),
+            pl.BlockSpec(memory_space=pltpu.HBM),
+            pl.BlockSpec(memory_space=pltpu.HBM),
         ],
         out_specs=pl.BlockSpec(memory_space=pltpu.VMEM),
         scratch_shapes=[
-            pltpu.VMEM((NZ, NX, ROWS, D), jnp.bfloat16),
+            pltpu.VMEM((1, NB), jnp.int32),
+            pltpu.VMEM((POOL, CAP, BS, 2 * D), jnp.bfloat16),
+            pltpu.VMEM((NZ, NX, REQ, HEADS, D), jnp.bfloat16),
             pltpu.VMEM((POOL * CAP, BS, 2 * D), jnp.bfloat16),
             pltpu.VMEM((POOL * CAP, BS, 2 * D), jnp.bfloat16),
             pltpu.VMEM((2 * NB, BS, 2 * D), jnp.bfloat16),
@@ -292,6 +306,7 @@
             dma((len(SPLIT), len(PEERS))),
             dma((len(SPLIT), len(PEERS))),
             dma((len(SPLIT),)),
+            dma((2,)),
             dma,
             dma,
             dma,
@@ -305,7 +320,7 @@
             dma((NZ,)),
         ],
         compiler_params=pltpu.CompilerParams(
-            collective_id=0, has_side_effects=True, vmem_limit_bytes=48 * 1024 * 1024
+            collective_id=0, has_side_effects=True, vmem_limit_bytes=63 * 1024 * 1024
         ),
         cost_estimate=pl.CostEstimate(flops=3_300_000_000, bytes_accessed=4_000_000, transcendentals=6_300_000),
     )(queries, kv_cache, block_owner.reshape(1, NB))

time: 49.7 us -> 47.5 us (0.956)
  local copies, waits for them, and re-layouts: 3.44 us -> 1.38 us
  Pallas kernels: 46.1 us -> 45.5 us
    unnamed x7 -> x1, local copies, waits for them, and re-layouts: 3.44 us -> 1.38 us
    pallas_call x1, Pallas kernels: 46.1 us -> 45.5 us  [body(): pl.pallas_call(kernel, out_shape=jax.ShapeDtypeStruct(queries.shape, quer...]
where the time goes in v2:
time: 47.5 us; the launch traced here: 46.9 us
  Pallas kernels  45.5 us (96%)
  local copies, waits for them, and re-layouts  1.38 us (3%)
    pallas_call x1, Pallas kernels, body(): pl.pallas_call(kernel, out_shape=jax.ShapeDtypeStruct(queries.shape, quer...  45.5 us
    unnamed x1, local copies, waits for them, and re-layouts  1.38 us

profile of v2, /device:TPU:4, one launch (start us, length us, event | category | flops | bytes accessed | tf_op | source)
XLA Modules:
  0.0 46.9 jit_solution(14080011142154214894)
XLA Ops:
  0.0 45.5 %shard_map.37 = bf16[8,16,128]{2,1,0:T(8,128)(2,1)} custom-call(bf16[8,16,128]{2,1,0:T(8,128)(2,1)} %q_ref.1, bf16[8,24,16,256]{3,2,1,0:T(8,128)(2,1)} %kv_ref.1, s32[1,96]{1,0:T(1,128)} %bitcast.1), custom_call_target="tpu_custom_call" | custom-call | flops 3300000000 | bytes 4000000 | tf_op jit(solution)/shard_map/pallas_call | solution.py:279
  45.5 1.4 %copy.5 = bf16[8,16,128]{2,1,0:T(8,128)(2,1)} copy(bf16[8,16,128]{2,1,0:T(8,128)(2,1)} %shard_map.37) | data formatting | bytes 65536

commit v3 on v2

--- a/solution.py
+++ b/solution.py
@@ -122,8 +122,8 @@
         start += size
         if m == 0:
             send_rows(0)
-    qx.wait_recv()
-    send_rows(1)
+            qx.wait_recv()
+            send_rows(1)
     owners_in.wait()
     packing(owner_v, table_v)
     to_smem = pltpu.make_async_copy(table_v, table_s, table_sem)
@@ -278,7 +278,7 @@
     dma = pltpu.SemaphoreType.DMA
     return pl.pallas_call(
         kernel,
-        out_shape=jax.ShapeDtypeStruct(queries.shape, queries.dtype),
+        out_shape=pltpu.VMEM(queries.shape, queries.dtype),
         in_specs=[
             pl.BlockSpec(memory_space=pltpu.HBM),
             pl.BlockSpec(memory_space=pltpu.HBM),
@@ -320,7 +320,7 @@
             dma((NZ,)),
         ],
         compiler_params=pltpu.CompilerParams(
-            collective_id=0, has_side_effects=True, vmem_limit_bytes=63 * 1024 * 1024
+            collective_id=0, has_side_effects=True, vmem_limit_bytes=56 * 1024 * 1024
         ),
         cost_estimate=pl.CostEstimate(flops=3_300_000_000, bytes_accessed=4_000_000, transcendentals=6_300_000),
     )(queries, kv_cache, block_owner.reshape(1, NB))

time: 47.5 us -> 46 us (0.968)
  local copies, waits for them, and re-layouts: 1.38 us -> 0.62 us
  Pallas kernels: 45.5 us -> 44.9 us
    unnamed x1, local copies, waits for them, and re-layouts: 1.38 us -> 0.62 us
    pallas_call x1, Pallas kernels: 45.5 us -> 44.9 us  [body(): pl.pallas_call(kernel, out_shape=pltpu.VMEM(queries.shape, queries.dtype)...]
where the time goes in v3:
time: 46 us; the launch traced here: 45.5 us
  Pallas kernels  44.9 us (98%)
  local copies, waits for them, and re-layouts  0.62 us (1%)
    pallas_call x1, Pallas kernels, body(): pl.pallas_call(kernel, out_shape=pltpu.VMEM(queries.shape, queries.dtype)...  44.9 us

profile of v3, /device:TPU:4, one launch (start us, length us, event | category | flops | bytes accessed | tf_op | source)
XLA Modules:
  0.0 45.5 jit_solution(16619076536412525350)
XLA Ops:
  0.0 44.9 %shard_map.37 = bf16[8,16,128]{2,1,0:T(8,128)(2,1)S(1)} custom-call(bf16[8,16,128]{2,1,0:T(8,128)(2,1)} %q_ref.1, bf16[8,24,16,256]{3,2,1,0:T(8,128)(2,1)} %kv_ref.1, s32[1,96]{1,0:T(1,128)} %bitcast.1), custom_call_target="tpu_custom_call" | custom-call | flops 3300000000 | bytes 4000000 | tf_op jit(solution)/shard_map/pallas_call | solution.py:279
  44.9 0.6 %copy.5 = bf16[8,16,128]{2,1,0:T(8,128)(2,1)} copy(bf16[8,16,128]{2,1,0:T(8,128)(2,1)S(1)} %shard_map.37) | data formatting | bytes 65536

commit v4 on v3

--- a/solution.py
+++ b/solution.py
@@ -218,9 +218,6 @@
             if i + 1 < TILES:
                 score(tiles[i + 1], (i + 1) % 2)
             soft(t, i % 2)
-            if final and i >= 1:
-                combine(2 * tiles[i - 1] + 1)
-                combine(2 * tiles[i - 1])
 
     swaps = []
     start = 0
@@ -247,8 +244,8 @@
         start += size
     swaps[-1].wait_recv()
     attend(len(SPLIT), base + blocks, blocks, final=True)
-    combine(1)
-    combine(0)
+    for s in range(NZ - 1, -1, -1):
+        combine(s)
 
     values, logs = [], []
     for s in range(NZ):

time: 46 us -> 45.5 us (0.989)
  no operation moved by 1% of the time
where the time goes in v4:
time: 45.5 us; the launch traced here: 45.4 us
  Pallas kernels  44.8 us (98%)
  local copies, waits for them, and re-layouts  0.62 us (1%)
    pallas_call x1, Pallas kernels, body(): pl.pallas_call(kernel, out_shape=pltpu.VMEM(queries.shape, queries.dtype)...  44.8 us

profile of v4, /device:TPU:4, one launch (start us, length us, event | category | flops | bytes accessed | tf_op | source)
XLA Modules:
  0.0 45.4 jit_solution(10684563822731390215)
XLA Ops:
  0.0 44.8 %shard_map.37 = bf16[8,16,128]{2,1,0:T(8,128)(2,1)S(1)} custom-call(bf16[8,16,128]{2,1,0:T(8,128)(2,1)} %q_ref.1, bf16[8,24,16,256]{3,2,1,0:T(8,128)(2,1)} %kv_ref.1, s32[1,96]{1,0:T(1,128)} %bitcast.1), custom_call_target="tpu_custom_call" | custom-call | flops 3300000000 | bytes 4000000 | tf_op jit(solution)/shard_map/pallas_call | solution.py:276
  44.8 0.6 %copy.5 = bf16[8,16,128]{2,1,0:T(8,128)(2,1)} copy(bf16[8,16,128]{2,1,0:T(8,128)(2,1)S(1)} %shard_map.37) | data formatting | bytes 65536

commit v5 on v4

--- a/solution.py
+++ b/solution.py
@@ -16,7 +16,7 @@
 NB, CAP = 96, 24
 REQ, HEADS = 8, 16
 ROWS = REQ * HEADS
-SPLIT = (8, 8, 8)
+SPLIT = (8, 6, 6, 4)
 PEERS = ((1, 2), (1, 1), (1, 3), (1, 0), (0, 2), (0, 1), (0, 3))
 PAIR = 2 * NX * ROWS
 TILES = NZ // 2

time: 45.5 us -> 45.3 us (level)
  no operation moved by 1% of the time
where the time goes in v5:
time: 45.3 us; the launch traced here: 45.2 us
  Pallas kernels  44.5 us (98%)
  local copies, waits for them, and re-layouts  0.62 us (1%)
    pallas_call x1, Pallas kernels, body(): pl.pallas_call(kernel, out_shape=pltpu.VMEM(queries.shape, queries.dtype)...  44.5 us

profile of v5, /device:TPU:4, one launch (start us, length us, event | category | flops | bytes accessed | tf_op | source)
XLA Modules:
  0.0 45.2 jit_solution(10513573549266683063)
XLA Ops:
  0.0 44.5 %shard_map.37 = bf16[8,16,128]{2,1,0:T(8,128)(2,1)S(1)} custom-call(bf16[8,16,128]{2,1,0:T(8,128)(2,1)} %q_ref.1, bf16[8,24,16,256]{3,2,1,0:T(8,128)(2,1)} %kv_ref.1, s32[1,96]{1,0:T(1,128)} %bitcast.1), custom_call_target="tpu_custom_call" | custom-call | flops 3300000000 | bytes 4000000 | tf_op jit(solution)/shard_map/pallas_call | solution.py:276
  44.6 0.6 %copy.5 = bf16[8,16,128]{2,1,0:T(8,128)(2,1)} copy(bf16[8,16,128]{2,1,0:T(8,128)(2,1)S(1)} %shard_map.37) | data formatting | bytes 65536
